TPU v7x, 32 devices: a whole 2x2x4 slice. The times are simulated.
32 devices in a mesh: spec: 4 (over x, core), space: 8 (over z, y).
Axes of the slice: x: 2, y: 2, z: 4, core: 2. Of those that a mesh axis runs over, the one named last changes fastest.
Arguments:
- spectra: float32 [768, 32, 128], P(None, ('space', 'spec')), may hold values from -6 to 6
- quad_first: bfloat16 [768, 768], replicated, may hold values from -0.21875 to 0.21875
- quad_second: bfloat16 [768, 768], replicated, may hold values from -0.21875 to 0.21875
- quad_output: bfloat16 [768, 768], replicated, may hold values from -0.21875 to 0.21875
- owner_map: int32 [8], replicated, may hold values from 0 to 2
- land_mask: int32 [32, 128], P('space'), may hold values 0 or 1
- nest_dest: int32 [512], P('space'), may hold values from 0 to 7, as said below
- nest_src: int32 [512], P('space'), may hold values from 0 to 511
- nest_into: int32 [512], P('space'), may hold values from 0 to 511
Outputs:
- spectra_out: float32 [768, 32, 128], P(None, ('space', 'spec'))
Inputs may be any that keep to these rules, and one draw needn't show every extreme that they name: `nest_dest`: among the 64 entries of each tile no tile is named more than 16 times, and one tile is named exactly 16 times by the entries of every tile.
All inputs are finite; a program needn't handle non-finite values. No bound on the sum of `land_mask` on one device may be relied on, other than what follows from the above.
Results may differ from a plain program's by a relative error of at most 0.0016.
Values sent between devices are 32-bit elements; how exact they have to be, the bound alone decides.
A program may use at most 64 MiB of HBM per device.

v0:
```python
import math

import jax
import jax.numpy as jnp
from jax import lax
from jax.sharding import PartitionSpec as P

DIRS = 24
SUBSTEPS = 6
CAP = 16
FREQS = 32


step_weight = 0.25
grid_factors = (1.0, 0.55, 0.3)


def padded_2(value, sides, width):
    for axis, dim in sides:
        devices, length = (lax.axis_size(axis), value.shape[dim])
        up = [(i, (i + 1) % devices) for i in range(devices - 1)]
        down = [(j, i) for i, j in up]
        last = lax.slice_in_dim(value, length - width, length, axis=dim)
        leading = lax.slice_in_dim(value, 0, width, axis=dim)
        before = lax.ppermute(last, axis, up)
        after = lax.ppermute(leading, axis, down)
        value = jnp.concatenate([before, value, after], axis=dim)
    return value


def minmod(lower_diff, upper_diff):
    return (
        0.5
        * (jnp.sign(lower_diff) + jnp.sign(upper_diff))
        * jnp.minimum(jnp.abs(lower_diff), jnp.abs(upper_diff))
    )


def upwind_sweep(padded, courant, forward, axis_index):
    length = padded.shape[axis_index]
    differences = lax.slice_in_dim(padded, 1, length, axis=axis_index) - lax.slice_in_dim(
        padded, 0, length - 1, axis=axis_index
    )
    slopes = minmod(
        lax.slice_in_dim(differences, 0, length - 2, axis=axis_index),
        lax.slice_in_dim(differences, 1, length - 1, axis=axis_index),
    )
    centres = lax.slice_in_dim(padded, 1, length - 1, axis=axis_index)
    upper_flux = courant * (centres + 0.5 * (1.0 - courant) * slopes)
    lower_flux = courant * (centres - 0.5 * (1.0 + courant) * slopes)
    face_count = length - 3
    fluxes = jnp.where(
        forward,
        lax.slice_in_dim(upper_flux, 0, face_count, axis=axis_index),
        lax.slice_in_dim(lower_flux, 1, face_count + 1, axis=axis_index),
    )
    interior = lax.slice_in_dim(padded, 2, length - 2, axis=axis_index)
    return interior - (
        lax.slice_in_dim(fluxes, 1, face_count, axis=axis_index)
        - lax.slice_in_dim(fluxes, 0, face_count - 1, axis=axis_index)
    )


def bin_speeds(first_bin, bin_count):
    indices = first_bin + jnp.arange(bin_count, dtype=jnp.int32)
    freq_index = (indices // DIRS).astype(jnp.float32)
    direction = ((indices % DIRS).astype(jnp.float32) + 0.5) * (2.0 * math.pi / DIRS)
    speeds = 0.2 + 0.7 * (freq_index + 0.5) / FREQS
    return (speeds * jnp.cos(direction), speeds * jnp.sin(direction))


def row_scales(owner_map, first_row, row_count, tile_rows):
    rows_here = first_row + jnp.arange(row_count, dtype=jnp.int32)
    tile_of = jnp.clip(rows_here // tile_rows, 0, owner_map.shape[0] - 1)
    matches = tile_of[:, None] == jnp.arange(owner_map.shape[0], dtype=jnp.int32)[None, :]
    grid_of = jnp.sum(jnp.where(matches, owner_map[None, :], 0), axis=1)
    scales = jnp.where(
        grid_of == 0, grid_factors[0], jnp.where(grid_of == 1, grid_factors[1], grid_factors[2])
    )
    return scales.astype(jnp.float32)


def substep(padded, scales, sea_rows, north_speed, east_speed):
    lat_courant = north_speed[:, None, None] * scales[None, 1:-1, None]
    advected = upwind_sweep(padded, lat_courant, (north_speed > 0)[:, None, None], 1)
    lon_padded = jnp.concatenate([advected[:, :, -2:], advected, advected[:, :, :2]], axis=2)
    lon_courant = east_speed[:, None, None] * scales[None, 2:-2, None]
    advected = upwind_sweep(lon_padded, lon_courant, (east_speed > 0)[:, None, None], 2)
    return advected * sea_rows[None]


def source_update(state_field, quad_first, quad_second, quad_output):
    contract = (((0,), (0,)), ((), ()))
    outline = state_field.shape
    matrix = state_field.reshape(outline[0], -1)
    rounded = matrix.astype(jnp.bfloat16)
    linear_one = lax.dot_general(quad_first, rounded, contract, preferred_element_type=jnp.float32)
    linear_two = lax.dot_general(quad_second, rounded, contract, preferred_element_type=jnp.float32)
    product = (linear_one * linear_two).astype(jnp.bfloat16)
    tendency = lax.dot_general(quad_output, product, contract, preferred_element_type=jnp.float32)
    return (matrix + step_weight * tendency).reshape(outline)


def shards(
    spectra,
    quad_first,
    quad_second,
    quad_output,
    owner_map,
    land_mask,
    nest_dest,
    nest_src,
    nest_into,
):
    spec_count = lax.axis_size("spec")
    tile_count = lax.axis_size("space")
    spec_rank = lax.axis_index("spec")
    tile_rank = lax.axis_index("space")
    lon_cols = spectra.shape[2]
    band_bins = spectra.shape[0] // spec_count
    sea_tile = land_mask.astype(jnp.float32)
    own_row = lax.dynamic_slice_in_dim(sea_tile, spec_rank, 1, 0)
    sourced = source_update(spectra, quad_first, quad_second, quad_output) * own_row[None]
    banded = lax.all_to_all(sourced, "spec", split_axis=0, concat_axis=1, tiled=True)
    north_speed, east_speed = bin_speeds(spec_rank * band_bins, band_bins)
    top_row = tile_rank * spec_count
    scales = row_scales(owner_map, top_row - 2, spec_count + 4, spec_count)
    for counter in range(SUBSTEPS):
        padded = padded_2(banded, (("space", 1),), 2)
        banded = substep(padded, scales, sea_tile, north_speed, east_speed)
    points = spec_count * lon_cols
    flat_field = banded.reshape(band_bins, points)
    slot_total = tile_count * CAP
    onehot = (nest_dest[:, None] == jnp.arange(tile_count, dtype=jnp.int32)[None, :]).astype(
        jnp.int32
    )
    slot_rank = jnp.sum(jnp.cumsum(onehot, axis=0) * onehot, axis=1) - 1
    slot_place = nest_dest * CAP + slot_rank
    outgoing = (
        jnp.zeros((band_bins, slot_total), jnp.float32)
        .at[:, slot_place]
        .set(flat_field[:, nest_src])
    )
    targets = jnp.full((1, slot_total), -1, jnp.int32).at[0, slot_place].set(nest_into)
    received, landing = (
        lax.all_to_all(outgoing, "space", split_axis=1, concat_axis=1, tiled=True),
        lax.all_to_all(targets, "space", split_axis=1, concat_axis=1, tiled=True),
    )
    usable = landing[0] >= 0
    target_point = jnp.where(usable, landing[0], 0)
    weights = usable.astype(jnp.float32)
    totals = (
        jnp.zeros((band_bins, points), jnp.float32)
        .at[:, target_point]
        .add(received * weights[None, :])
    )
    counts = jnp.zeros((points,), jnp.float32).at[target_point].add(weights)
    merged = (flat_field + totals) / (1.0 + counts)[None, :]
    finished = source_update(
        lax.all_to_all(
            merged.reshape(band_bins, spec_count, lon_cols),
            "spec",
            split_axis=1,
            concat_axis=0,
            tiled=True,
        ),
        quad_first,
        quad_second,
        quad_output,
    )
    return finished * own_row[None]


def solution(mesh):
    return jax.shard_map(
        shards,
        mesh=mesh,
        in_specs=(
            P(None, ("space", "spec"), None),
            P(),
            P(),
            P(),
            P(),
            P("space", None),
            P("space"),
            P("space"),
            P("space"),
        ),
        out_specs=P(None, ("space", "spec"), None),
        check_vma=False,
    )
```

profile of v0, /device:TPU:0, one launch (start us, length us, event | category | flops | bytes accessed | tf_op | source)
XLA Modules:
  0.0 163.2 jit_solution(3121085591942889693)
XLA Ops:
  0.0 0.8 convert_element_type.63
  0.8 2.0 %copy.28 = f32[768,1,128]{0,2,1:T(8,128)} copy(f32[768,1,128]{2,1,0:T(1,128)} %param.9) | data formatting | bytes 786432 | tf_op args[0]
  2.8 2.3 %fusion.102 = f32[768,128]{1,0:T(8,128)} fusion(bf16[768,768]{1,0:T(8,128)(2,1)S(1)} %copy-done, f32[768,1,128]{0,2,1:T(8,128)} %copy.28), kind=kOutput, calls=%fused_computation.238 | convolution fusion | flops 150994944 | bytes 1966080 | tf_op jit(solution)/shard_map/dot_general | solution.py:97
  5.1 3.1 %fusion.4 = f32[768,1,128]{0,2,1:T(8,128)} fusion(bf16[768,768]{1,0:T(8,128)(2,1)S(1)} %copy-done.1, f32[768,128]{1,0:T(8,128)} %fusion.102, bf16[768,768]{1,0:T(8,128)(2,1)S(1)} %copy-done.2, f32[768,1,128]{0,2,1:T(8,128)} %copy.28, f32[128]{0:T(128)S(1)} %dynamic-slice_bitcast_fusion), kind=kOutput, calls=%fused_computation.13 | convolution fusion | flops 302481408 | bytes 3539456 | tf_op jit(solution)/shard_map/dot_general | solution.py:100
  8.2 1.9 %copy.29 = f32[768,1,128]{2,1,0:T(1,128)} copy(f32[768,1,128]{0,2,1:T(8,128)} %fusion.4) | data formatting | bytes 786432 | tf_op jit(solution)/shard_map/mul | solution.py:123
  10.1 4.2 %all-to-all-start = ((f32[768,1,128]{2,1,0:T(1,128)}), f32[768,1,128]{2,1,0:T(1,128)S(1)}, u32[]{:S(2)}, u32[]{:S(2)}) async-start(f32[768,1,128]{2,1,0:T(1,128)} %copy.29), calls=%async_computation | async-start | bytes 786432 | tf_op jit(solution)/shard_map/all_to_all | solution.py:124
  14.9 6.8 %all-to-all-done = f32[768,1,128]{2,1,0:T(1,128)S(1)} async-done(((f32[768,1,128]{2,1,0:T(1,128)}), f32[768,1,128]{2,1,0:T(1,128)S(1)}, u32[]{:S(2)}, u32[]{:S(2)}) %all-to-all-start) | async-done | bytes 393248 | tf_op jit(solution)/shard_map/all_to_all | solution.py:124
  21.8 4.1 %collective-permute-start = (f32[192,2,128]{2,0,1:T(8,128)S(1)}, f32[192,2,128]{2,0,1:T(8,128)S(1)}, u32[]{:S(2)}, u32[]{:S(2)}) collective-permute-start(f32[192,2,128]{2,0,1:T(8,128)S(1)} %get-tuple-element.27), channel_id=1, source_target_pairs={{0,1},{1,2},{2,3},{3,4},{4,5},{5,6},{6,7},{8,9},{9,10},{10,11},{11... | collective-permute-start | bytes 589832 | tf_op jit(solution)/shard_map/ppermute | solution.py:25
  25.9 1.3 collective-permute-start.1
  27.2 2.6 %collective-permute-done = f32[192,2,128]{2,0,1:T(8,128)S(1)} collective-permute-done((f32[192,2,128]{2,0,1:T(8,128)S(1)}, f32[192,2,128]{2,0,1:T(8,128)S(1)}, u32[]{:S(2)}, u32[]{:S(2)}) %collective-permute-start) | collective-permute-done | bytes 196640 | tf_op jit(solution)/shard_map/ppermute | solution.py:25
  29.9 4.1 %collective-permute-done.1 = f32[192,2,128]{2,0,1:T(8,128)S(1)} collective-permute-done((f32[192,2,128]{2,0,1:T(8,128)S(1)}, f32[192,2,128]{2,0,1:T(8,128)S(1)}, u32[]{:S(2)}, u32[]{:S(2)}) %collective-permute-start.1) | collective-permute-done | bytes 196640 | tf_op jit(solution)/shard_map/ppermute | solution.py:26
  36.8 0.8 fusion.26
  37.9 4.5 %collective-permute-start.2 = (f32[192,2,128]{2,0,1:T(8,128)S(1)}, f32[192,2,128]{2,0,1:T(8,128)S(1)}, u32[]{:S(2)}, u32[]{:S(2)}) collective-permute-start(f32[192,2,128]{2,0,1:T(8,128)S(1)} %get-tuple-element.23), channel_id=1, source_target_pairs={{0,1},{1,2},{2,3},{3,4},{4,5},{5,6},{6,7},{8,9},{9,10},{10,11},{11... | collective-permute-start | bytes 589832 | tf_op jit(solution)/shard_map/ppermute | solution.py:25
  42.4 1.3 collective-permute-start.3
  43.7 1.9 %collective-permute-done.2 = f32[192,2,128]{2,0,1:T(8,128)S(1)} collective-permute-done((f32[192,2,128]{2,0,1:T(8,128)S(1)}, f32[192,2,128]{2,0,1:T(8,128)S(1)}, u32[]{:S(2)}, u32[]{:S(2)}) %collective-permute-start.2) | collective-permute-done | bytes 196640 | tf_op jit(solution)/shard_map/ppermute | solution.py:25
  45.5 6.0 %collective-permute-done.3 = f32[192,2,128]{2,0,1:T(8,128)S(1)} collective-permute-done((f32[192,2,128]{2,0,1:T(8,128)S(1)}, f32[192,2,128]{2,0,1:T(8,128)S(1)}, u32[]{:S(2)}, u32[]{:S(2)}) %collective-permute-start.3) | collective-permute-done | bytes 196640 | tf_op jit(solution)/shard_map/ppermute | solution.py:26
  51.9 0.7 fusion.41
  54.4 0.8 fusion.23
  56.1 4.5 %collective-permute-start.4 = (f32[192,2,128]{2,0,1:T(8,128)}, f32[192,2,128]{2,0,1:T(8,128)S(1)}, u32[]{:S(2)}, u32[]{:S(2)}) collective-permute-start(f32[192,2,128]{2,0,1:T(8,128)} %get-tuple-element.19), channel_id=1, source_target_pairs={{0,1},{1,2},{2,3},{3,4},{4,5},{5,6},{6,7},{8,9},{9,10},{10,11},{11... | collective-permute-start | bytes 589832 | tf_op jit(solution)/shard_map/ppermute | solution.py:25
  60.6 1.5 collective-permute-start.5
  62.5 1.6 %collective-permute-done.4 = f32[192,2,128]{2,0,1:T(8,128)S(1)} collective-permute-done((f32[192,2,128]{2,0,1:T(8,128)}, f32[192,2,128]{2,0,1:T(8,128)S(1)}, u32[]{:S(2)}, u32[]{:S(2)}) %collective-permute-start.4) | collective-permute-done | bytes 196640 | tf_op jit(solution)/shard_map/ppermute | solution.py:25
  64.1 5.8 %collective-permute-done.5 = f32[192,2,128]{2,0,1:T(8,128)S(1)} collective-permute-done((f32[192,2,128]{2,0,1:T(8,128)S(1)}, f32[192,2,128]{2,0,1:T(8,128)S(1)}, u32[]{:S(2)}, u32[]{:S(2)}) %collective-permute-start.5) | collective-permute-done | bytes 196640 | tf_op jit(solution)/shard_map/ppermute | solution.py:26
  72.8 0.8 fusion.20
  74.5 4.5 %collective-permute-start.6 = (f32[192,2,128]{2,0,1:T(8,128)}, f32[192,2,128]{2,0,1:T(8,128)S(1)}, u32[]{:S(2)}, u32[]{:S(2)}) collective-permute-start(f32[192,2,128]{2,0,1:T(8,128)} %get-tuple-element.15), channel_id=1, source_target_pairs={{0,1},{1,2},{2,3},{3,4},{4,5},{5,6},{6,7},{8,9},{9,10},{10,11},{11... | collective-permute-start | bytes 589832 | tf_op jit(solution)/shard_map/ppermute | solution.py:25
  79.1 1.3 collective-permute-start.7
  80.4 0.9 scatter_custom_fusion
  82.0 8.2 %all-to-all-start.1 = ((s32[1,8,16]{2,0,1:T(1,128)}), s32[1,8,16]{2,0,1:T(1,128)S(1)}, u32[]{:S(2)}, u32[]{:S(2)}) async-start(s32[1,8,16]{2,0,1:T(1,128)} %bitcast.10), calls=%async_computation.1 | async-start | bytes 8192 | tf_op jit(solution)/shard_map/all_to_all | solution.py:147
  90.6 0.7 fusion.35
  93.0 0.8 fusion.17
  94.1 3.9 %collective-permute-start.8 = (f32[192,2,128]{2,0,1:T(8,128)S(1)}, f32[192,2,128]{2,0,1:T(8,128)S(1)}, u32[]{:S(2)}, u32[]{:S(2)}) collective-permute-start(f32[192,2,128]{2,0,1:T(8,128)S(1)} %get-tuple-element.11), channel_id=1, source_target_pairs={{0,1},{1,2},{2,3},{3,4},{4,5},{5,6},{6,7},{8,9},{9,10},{10,11},{11... | collective-permute-start | bytes 589832 | tf_op jit(solution)/shard_map/ppermute | solution.py:25
  98.0 1.3 collective-permute-start.9
  99.4 1.9 %collective-permute-done.8 = f32[192,2,128]{2,0,1:T(8,128)S(1)} collective-permute-done((f32[192,2,128]{2,0,1:T(8,128)S(1)}, f32[192,2,128]{2,0,1:T(8,128)S(1)}, u32[]{:S(2)}, u32[]{:S(2)}) %collective-permute-start.8) | collective-permute-done | bytes 196640 | tf_op jit(solution)/shard_map/ppermute | solution.py:25
  101.2 5.3 %collective-permute-done.9 = f32[192,2,128]{2,0,1:T(8,128)S(1)} collective-permute-done((f32[192,2,128]{2,0,1:T(8,128)S(1)}, f32[192,2,128]{2,0,1:T(8,128)S(1)}, u32[]{:S(2)}, u32[]{:S(2)}) %collective-permute-start.9) | collective-permute-done | bytes 196640 | tf_op jit(solution)/shard_map/ppermute | solution.py:26
  109.4 0.8 fusion.14
  111.2 4.5 %collective-permute-start.10 = (f32[192,2,128]{2,0,1:T(8,128)}, f32[192,2,128]{2,0,1:T(8,128)S(1)}, u32[]{:S(2)}, u32[]{:S(2)}) collective-permute-start(f32[192,2,128]{2,0,1:T(8,128)} %get-tuple-element.7), channel_id=1, source_target_pairs={{0,1},{1,2},{2,3},{3,4},{4,5},{5,6},{6,7},{8,9},{9,10},{10,11},{11... | collective-permute-start | bytes 589832 | tf_op jit(solution)/shard_map/ppermute | solution.py:25
  115.7 1.5 collective-permute-start.11
  119.2 5.8 %collective-permute-done.11 = f32[192,2,128]{2,0,1:T(8,128)S(1)} collective-permute-done((f32[192,2,128]{2,0,1:T(8,128)S(1)}, f32[192,2,128]{2,0,1:T(8,128)S(1)}, u32[]{:S(2)}, u32[]{:S(2)}) %collective-permute-start.11) | collective-permute-done | bytes 196640 | tf_op jit(solution)/shard_map/ppermute | solution.py:26
  127.9 0.8 fusion.11
  129.1 1.6 scatter_custom_fusion.1
  130.7 7.3 %all-to-all-start.2 = ((f32[192,8,16]{0,2,1:T(8,128)}), f32[192,8,16]{0,2,1:T(8,128)S(1)}, u32[]{:S(2)}, u32[]{:S(2)}) async-start(f32[192,8,16]{0,2,1:T(8,128)} %bitcast.12), calls=%async_computation.2 | async-start | bytes 262144 | tf_op jit(solution)/shard_map/all_to_all | solution.py:146
  138.0 1.4 scatter_custom_fusion.3
  139.4 5.9 %all-to-all-done.2 = f32[192,8,16]{0,2,1:T(8,128)S(1)} async-done(((f32[192,8,16]{0,2,1:T(8,128)}), f32[192,8,16]{0,2,1:T(8,128)S(1)}, u32[]{:S(2)}, u32[]{:S(2)}) %all-to-all-start.2) | async-done | bytes 98336 | tf_op jit(solution)/shard_map/all_to_all | solution.py:146
  145.4 1.5 scatter_custom_fusion.2
  147.1 0.9 copy.32
  148.0 10.9 %all_to_all.54 = f32[192,4,128]{2,0,1:T(8,128)S(1)} all-to-all(f32[192,4,128]{2,0,1:T(8,128)} %copy.32), channel_id=1, replica_groups=mesh['spec'=4,'space'=8] {'spec'}, dimensions={1} | all-to-all | bytes 786432 | tf_op jit(solution)/shard_map/all_to_all | solution.py:160
  159.0 1.1 fusion.69
  160.1 2.0 %fusion.7 = f32[768,1,128]{0,2,1:T(8,128)S(1)} fusion(f32[768,128]{0,1:T(8,128)S(1)} %copy.33, bf16[768,768]{1,0:T(8,128)(2,1)S(1)} %copy-done.1, f32[128,768]{1,0:T(8,128)} %fusion.69, bf16[768,768]{1,0:T(8,128)(2,1)} %param.11, f32[128]{0:T(128)S(1)} %dynamic-slice_bitcast_fusion, f32[768,128]{1,0:T(8,128)S(1)} %bitcast.71), kind=kOutput, calls=%fused_computation.16 | convolution fusion | flops 302579712 | bytes 3932672 | tf_op jit(solution)/shard_map/dot_general | solution.py:100
  162.2 1.0 copy.34
  (122 shorter events, 23.0 us)
Async XLA Ops:
  0.0 2.8 %copy-start = (bf16[768,768]{1,0:T(8,128)(2,1)S(1)}, bf16[768,768]{1,0:T(8,128)(2,1)}, u32[]{:S(2)}) copy-start(bf16[768,768]{1,0:T(8,128)(2,1)} %param.10) | copy-start | bytes 3538948
  0.8 4.3 %copy-start.2 = (bf16[768,768]{1,0:T(8,128)(2,1)S(1)}, bf16[768,768]{1,0:T(8,128)(2,1)}, u32[]{:S(2)}) copy-start(bf16[768,768]{1,0:T(8,128)(2,1)} %param.11) | copy-start | bytes 3538948
  2.8 2.4 %copy-start.1 = (bf16[768,768]{1,0:T(8,128)(2,1)S(1)}, bf16[768,768]{1,0:T(8,128)(2,1)}, u32[]{:S(2)}) copy-start(bf16[768,768]{1,0:T(8,128)(2,1)} %param.12) | copy-start | bytes 3538948
  8.2 6.2 %copy-start.4 = (s32[8]{0:T(128)S(1)}, s32[8]{0:T(128)}, u32[]{:S(2)}) copy-start(s32[8]{0:T(128)} %param.13) | copy-start | bytes 100
  10.1 11.7 %all-to-all-start = ((f32[768,1,128]{2,1,0:T(1,128)}), f32[768,1,128]{2,1,0:T(1,128)S(1)}, u32[]{:S(2)}, u32[]{:S(2)}) async-start(f32[768,1,128]{2,1,0:T(1,128)} %copy.29), calls=%async_computation | async-start | bytes 786432 | tf_op jit(solution)/shard_map/all_to_all | solution.py:124
  21.8 8.1 %collective-permute-start = (f32[192,2,128]{2,0,1:T(8,128)S(1)}, f32[192,2,128]{2,0,1:T(8,128)S(1)}, u32[]{:S(2)}, u32[]{:S(2)}) collective-permute-start(f32[192,2,128]{2,0,1:T(8,128)S(1)} %get-tuple-element.27), channel_id=1, source_target_pairs={{0,1},{1,2},{2,3},{3,4},{4,5},{5,6},{6,7},{8,9},{9,10},{10,11},{11... | collective-permute-start | bytes 589832 | tf_op jit(solution)/shard_map/ppermute | solution.py:25
  25.9 8.1 %collective-permute-start.1 = (f32[192,2,128]{2,0,1:T(8,128)S(1)}, f32[192,2,128]{2,0,1:T(8,128)S(1)}, u32[]{:S(2)}, u32[]{:S(2)}) collective-permute-start(f32[192,2,128]{2,0,1:T(8,128)S(1)} %get-tuple-element.28), channel_id=1, source_target_pairs={{1,0},{2,1},{3,2},{4,3},{5,4},{6,5},{7,6},{9,8},{10,9},{11,10},{12... | collective-permute-start | bytes 589832 | tf_op jit(solution)/shard_map/ppermute | solution.py:26
  37.9 7.7 %collective-permute-start.2 = (f32[192,2,128]{2,0,1:T(8,128)S(1)}, f32[192,2,128]{2,0,1:T(8,128)S(1)}, u32[]{:S(2)}, u32[]{:S(2)}) collective-permute-start(f32[192,2,128]{2,0,1:T(8,128)S(1)} %get-tuple-element.23), channel_id=1, source_target_pairs={{0,1},{1,2},{2,3},{3,4},{4,5},{5,6},{6,7},{8,9},{9,10},{10,11},{11... | collective-permute-start | bytes 589832 | tf_op jit(solution)/shard_map/ppermute | solution.py:25
  42.4 9.1 %collective-permute-start.3 = (f32[192,2,128]{2,0,1:T(8,128)S(1)}, f32[192,2,128]{2,0,1:T(8,128)S(1)}, u32[]{:S(2)}, u32[]{:S(2)}) collective-permute-start(f32[192,2,128]{2,0,1:T(8,128)S(1)} %get-tuple-element.24), channel_id=1, source_target_pairs={{1,0},{2,1},{3,2},{4,3},{5,4},{6,5},{7,6},{9,8},{10,9},{11,10},{12... | collective-permute-start | bytes 589832 | tf_op jit(solution)/shard_map/ppermute | solution.py:26
  55.2 6.9 %copy-start.3 = (s32[64]{0:T(128)S(1)}, s32[64]{0:T(128)}, u32[]{:S(2)}) copy-start(s32[64]{0:T(128)} %param.15) | copy-start | bytes 772
  56.1 8.0 %collective-permute-start.4 = (f32[192,2,128]{2,0,1:T(8,128)}, f32[192,2,128]{2,0,1:T(8,128)S(1)}, u32[]{:S(2)}, u32[]{:S(2)}) collective-permute-start(f32[192,2,128]{2,0,1:T(8,128)} %get-tuple-element.19), channel_id=1, source_target_pairs={{0,1},{1,2},{2,3},{3,4},{4,5},{5,6},{6,7},{8,9},{9,10},{10,11},{11... | collective-permute-start | bytes 589832 | tf_op jit(solution)/shard_map/ppermute | solution.py:25
  60.6 9.3 %collective-permute-start.5 = (f32[192,2,128]{2,0,1:T(8,128)S(1)}, f32[192,2,128]{2,0,1:T(8,128)S(1)}, u32[]{:S(2)}, u32[]{:S(2)}) collective-permute-start(f32[192,2,128]{2,0,1:T(8,128)S(1)} %get-tuple-element.20), channel_id=1, source_target_pairs={{1,0},{2,1},{3,2},{4,3},{5,4},{6,5},{7,6},{9,8},{10,9},{11,10},{12... | collective-permute-start | bytes 589832 | tf_op jit(solution)/shard_map/ppermute | solution.py:26
  74.5 15.6 %collective-permute-start.6 = (f32[192,2,128]{2,0,1:T(8,128)}, f32[192,2,128]{2,0,1:T(8,128)S(1)}, u32[]{:S(2)}, u32[]{:S(2)}) collective-permute-start(f32[192,2,128]{2,0,1:T(8,128)} %get-tuple-element.15), channel_id=1, source_target_pairs={{0,1},{1,2},{2,3},{3,4},{4,5},{5,6},{6,7},{8,9},{9,10},{10,11},{11... | collective-permute-start | bytes 589832 | tf_op jit(solution)/shard_map/ppermute | solution.py:25
  79.1 11.1 %collective-permute-start.7 = (f32[192,2,128]{2,0,1:T(8,128)S(1)}, f32[192,2,128]{2,0,1:T(8,128)S(1)}, u32[]{:S(2)}, u32[]{:S(2)}) collective-permute-start(f32[192,2,128]{2,0,1:T(8,128)S(1)} %get-tuple-element.16), channel_id=1, source_target_pairs={{1,0},{2,1},{3,2},{4,3},{5,4},{6,5},{7,6},{9,8},{10,9},{11,10},{12... | collective-permute-start | bytes 589832 | tf_op jit(solution)/shard_map/ppermute | solution.py:26
  82.0 35.3 %all-to-all-start.1 = ((s32[1,8,16]{2,0,1:T(1,128)}), s32[1,8,16]{2,0,1:T(1,128)S(1)}, u32[]{:S(2)}, u32[]{:S(2)}) async-start(s32[1,8,16]{2,0,1:T(1,128)} %bitcast.10), calls=%async_computation.1 | async-start | bytes 8192 | tf_op jit(solution)/shard_map/all_to_all | solution.py:147
  93.9 5.5 %copy-start.5 = (s32[64]{0:T(128)S(1)}, s32[64]{0:T(128)}, u32[]{:S(2)}) copy-start(s32[64]{0:T(128)} %param.16) | copy-start | bytes 772
  94.1 7.1 %collective-permute-start.8 = (f32[192,2,128]{2,0,1:T(8,128)S(1)}, f32[192,2,128]{2,0,1:T(8,128)S(1)}, u32[]{:S(2)}, u32[]{:S(2)}) collective-permute-start(f32[192,2,128]{2,0,1:T(8,128)S(1)} %get-tuple-element.11), channel_id=1, source_target_pairs={{0,1},{1,2},{2,3},{3,4},{4,5},{5,6},{6,7},{8,9},{9,10},{10,11},{11... | collective-permute-start | bytes 589832 | tf_op jit(solution)/shard_map/ppermute | solution.py:25
  98.0 8.5 %collective-permute-start.9 = (f32[192,2,128]{2,0,1:T(8,128)S(1)}, f32[192,2,128]{2,0,1:T(8,128)S(1)}, u32[]{:S(2)}, u32[]{:S(2)}) collective-permute-start(f32[192,2,128]{2,0,1:T(8,128)S(1)} %get-tuple-element.12), channel_id=1, source_target_pairs={{1,0},{2,1},{3,2},{4,3},{5,4},{6,5},{7,6},{9,8},{10,9},{11,10},{12... | collective-permute-start | bytes 589832 | tf_op jit(solution)/shard_map/ppermute | solution.py:26
  111.2 8.0 %collective-permute-start.10 = (f32[192,2,128]{2,0,1:T(8,128)}, f32[192,2,128]{2,0,1:T(8,128)S(1)}, u32[]{:S(2)}, u32[]{:S(2)}) collective-permute-start(f32[192,2,128]{2,0,1:T(8,128)} %get-tuple-element.7), channel_id=1, source_target_pairs={{0,1},{1,2},{2,3},{3,4},{4,5},{5,6},{6,7},{8,9},{9,10},{10,11},{11... | collective-permute-start | bytes 589832 | tf_op jit(solution)/shard_map/ppermute | solution.py:25
  115.7 9.3 %collective-permute-start.11 = (f32[192,2,128]{2,0,1:T(8,128)S(1)}, f32[192,2,128]{2,0,1:T(8,128)S(1)}, u32[]{:S(2)}, u32[]{:S(2)}) collective-permute-start(f32[192,2,128]{2,0,1:T(8,128)S(1)} %get-tuple-element.8), channel_id=1, source_target_pairs={{1,0},{2,1},{3,2},{4,3},{5,4},{6,5},{7,6},{9,8},{10,9},{11,10},{12... | collective-permute-start | bytes 589832 | tf_op jit(solution)/shard_map/ppermute | solution.py:26
  130.7 14.6 %all-to-all-start.2 = ((f32[192,8,16]{0,2,1:T(8,128)}), f32[192,8,16]{0,2,1:T(8,128)S(1)}, u32[]{:S(2)}, u32[]{:S(2)}) async-start(f32[192,8,16]{0,2,1:T(8,128)} %bitcast.12), calls=%async_computation.2 | async-start | bytes 262144 | tf_op jit(solution)/shard_map/all_to_all | solution.py:146
where the time goes:
time: 164 us; the launch traced here: 163 us
  starting transfers between devices  53.9 us (33%)
  waiting for transfers between devices  48.2 us (29%)
  other arithmetic  25.5 us (16%)
  local copies, waits for them, and re-layouts  15.4 us (9%)
  blocking collectives  10.9 us (7%)
  matrix products  8.53 us (5%)
    ppermute x6, waiting for transfers between devices, padded_2(): after = lax.ppermute(leading, axis, down)  27 us
    ppermute x6, starting transfers between devices, padded_2(): before = lax.ppermute(last, axis, up)  26.1 us
    all_to_all x1, blocking collectives, shards(): lax.all_to_all(merged.reshape(band_bins, spec_count, lon_cols), 'spec', s...  10.9 us
    select_n x12, other arithmetic, upwind_sweep(): jnp.where(forward, lax.slice_in_dim(upper_flux, 0, face_count, axis=axis_...  9.33 us
    ppermute x6, waiting for transfers between devices, padded_2(): before = lax.ppermute(last, axis, up)  8.51 us
    all_to_all x1, starting transfers between devices, shards(): lax.all_to_all(targets, 'space', split_axis=1, concat_axis=1, tiled=True)  8.16 us
    ppermute x6, starting transfers between devices, padded_2(): after = lax.ppermute(leading, axis, down)  8.15 us
    all_to_all x1, starting transfers between devices, shards(): lax.all_to_all(outgoing, 'space', split_axis=1, concat_axis=1, tiled=True)  7.26 us
  transfers between devices with their start and end apart: 15, of which 12 were waited for; matrix products, arithmetic and copies ran while one was open for 8% of the time, Pallas kernels for 0%

commit v1 on v0

v1 whole, which is shorter than its diff:
```python
import functools
import math

import jax
import jax.numpy as jnp
from jax import lax
from jax.experimental import pallas as pl
from jax.experimental.pallas import tpu as pltpu
from jax.sharding import PartitionSpec as P

DIRS = 24
SUBSTEPS = 6
FREQS = 32
PARTS = 1

step_weight = 0.25
grid_factors = (1.0, 0.55, 0.3)

F32 = jnp.float32
BF16 = jnp.bfloat16
MESH = pl.DeviceIdType.MESH


def minmod(a, b):
    return jnp.maximum(jnp.minimum(a, 0.0), jnp.minimum(b, jnp.maximum(a, 0.0)))


def split_high_low(x):
    high = x.astype(BF16)
    return high, (x - high.astype(F32)).astype(BF16)


def repeat(count, body):
    if count <= 4:
        for i in range(count):
            body(i)
    else:
        lax.fori_loop(0, count, lambda i, c: (body(i), c)[1], 0)


def kernel(
    dims,
    spectra, quad_first, quad_second, quad_output, owner, land, dest, src, into,
    out,
    field, w1, w2, w3, outbox, cells, inbox, meta, ent, mask_b, inv_b, coef, speed, oh_src, oh_dst, gathered,
    load_sem, meta_send, meta_recv, go_send, go_recv, back_send, back_recv,
):
    n, tiles, spec, bins, lon, band, parts, pband, entries = dims
    rows = n
    shift = lon.bit_length() - 1
    spec_rank = lax.axis_index("spec")
    tile = lax.axis_index("space")
    me = tile * spec + spec_rank

    loads = [
        pltpu.make_async_copy(a, b, load_sem.at[i])
        for i, (a, b) in enumerate(
            ((spectra, field), (quad_first, w1), (quad_second, w2), (quad_output, w3))
        )
    ]
    for copy in loads:
        copy.start()

    def target(q):
        return {"space": lax.div(q, spec), "spec": lax.rem(q, spec)}

    def peer(k):
        half = lax.div(k + 1, 2)
        offset = n // 2 + half * (1 - 2 * lax.rem(k, 2))
        return lax.rem(me + offset, n)

    barrier = pltpu.get_barrier_semaphore()

    def greet(k, c):
        pl.semaphore_signal(barrier, inc=1, device_id=target(peer(k)), device_id_type=MESH)
        return c

    lax.fori_loop(0, n - 1, greet, 0)

    width = min(entries, lon)
    per = lon // width
    erows = entries // width
    base = -(-spec // 8) * 8
    mine = jnp.zeros(meta.shape[1:], jnp.int32)
    meta[tile] = mine
    meta[tile, 0:spec, :] = land[...]
    for j, part in enumerate((dest, src, into)):
        meta[tile, base + j * erows : base + (j + 1) * erows, 0:width] = part[...]
    own_mask = land[pl.ds(spec_rank, 1), :].astype(F32)

    pl.semaphore_wait(barrier, n - 1)

    def meta_copy(k):
        return pltpu.make_async_remote_copy(
            src_ref=meta.at[tile],
            dst_ref=meta.at[tile],
            send_sem=meta_send,
            recv_sem=meta_recv,
            device_id={"space": lax.rem(tile + k, tiles), "spec": spec_rank},
            device_id_type=MESH,
        )

    def send_meta(k, c):
        meta_copy(k).start()
        return c

    lax.fori_loop(1, tiles, send_meta, 0)

    def source(x):
        xt = x.T.astype(BF16)
        one = jnp.dot(xt, w1[...], preferred_element_type=F32)
        two = jnp.dot(xt, w2[...], preferred_element_type=F32)
        product = (one * two).astype(BF16)
        tendency = jnp.dot(product, w3[...], preferred_element_type=F32)
        return x + step_weight * tendency.T

    for copy in loads:
        copy.wait()
    sourced = source(field[...]) * own_mask
    if band % 8 == 0:
        outbox[...] = sourced.reshape(n, parts, pband, lon)
    else:
        field[...] = sourced
        outbox[...] = jnp.zeros_like(outbox)
        for q in range(n):
            outbox[q, 0, 0:band, :] = field[q * band : (q + 1) * band, :]

    for p in range(parts):

        def send(k, c):
            q = peer(k)
            pltpu.make_async_remote_copy(
                src_ref=outbox.at[q, p],
                dst_ref=cells.at[p, me],
                send_sem=go_send.at[p],
                recv_sem=go_recv.at[p],
                device_id=target(q),
                device_id_type=MESH,
            ).start()
            return c

        lax.fori_loop(0, n - 1, send, 0)
        cells[p, me] = outbox[me, p]

    local = lax.broadcasted_iota(jnp.int32, (parts * pband, lon), 0)
    index = (local + me * band).astype(F32)
    freq = jnp.floor((index + 0.5) * (1.0 / DIRS))
    direction = (index - DIRS * freq + 0.5) * (2.0 * math.pi / DIRS)
    speeds = 0.2 + 0.7 * (freq + 0.5) / FREQS
    speed[0] = speeds * jnp.cos(direction)
    speed[1] = speeds * jnp.sin(direction)
    for t in range(tiles):
        grid = owner[t]
        factor = jnp.where(
            grid == 0, grid_factors[0], jnp.where(grid == 1, grid_factors[1], grid_factors[2])
        ).astype(F32)
        for axis in range(2):
            courant = speed[axis] * factor
            coef[2 * axis, t] = jnp.abs(courant)
            coef[2 * axis + 1, t] = 0.5 * courant * (1.0 - jnp.abs(courant))

    drained = pltpu.make_async_copy(
        meta.at[pl.ds(0, tiles - 1)], meta.at[pl.ds(0, tiles - 1)], meta_recv
    )
    drained.wait()
    lanes = lax.broadcasted_iota(jnp.int32, (1, lon), 1)
    for t in range(tiles):
        sea = meta[t, 0:spec, :].astype(F32)
        for r in range(spec):
            mask_b[t * spec + r] = jnp.broadcast_to(sea[r : r + 1, :], mask_b.shape[1:])
    for u in range(tiles * erows // per):
        packed = [jnp.zeros((1, lon), jnp.int32) for _ in range(4)]
        for v in range(per):
            t = (u * per + v) // erows
            line = (u * per + v) % erows
            d, s, i = (
                meta[t, base + j * erows + line : base + j * erows + line + 1, :] for j in range(3)
            )
            values = (
                t * spec + lax.shift_right_logical(s, shift),
                s & (lon - 1),
                d * spec + lax.shift_right_logical(i, shift),
                i & (lon - 1),
            )
            here = (lanes >= v * width) & (lanes < (v + 1) * width)
            for j in range(4):
                moved = pltpu.roll(values[j], v * width, 1) if v else values[j]
                packed[j] = jnp.where(here, moved, packed[j])
        for j in range(4):
            ent[j, u] = jnp.broadcast_to(packed[j], ent.shape[2:])

    chunk = oh_src.shape[2]
    lines = chunk // lon
    chunks = tiles * entries // chunk
    chunk_tiles = chunk // entries
    crows = chunk_tiles * spec

    def wide(j, c):
        return jnp.concatenate([ent[j, c * lines + v] for v in range(lines)], axis=1)

    def hots(c):
        column = lax.broadcasted_iota(jnp.int32, (lon, chunk), 0)
        one = jnp.where(column == wide(1, c)[0:1, :], 1.0, 0.0).astype(BF16)
        oh_src[c, 0:lon, :] = one
        oh_src[c, lon : 2 * lon, :] = one
        two = jnp.where(column == wide(3, c)[0:1, :], 1.0, 0.0).astype(BF16)
        oh_dst[c, :, 0:chunk] = two
        oh_dst[c, :, chunk : 2 * chunk] = two

    repeat(chunks, hots)
    contract_last = (((1,), (1,)), ((), ()))
    row_block = min(rows, 32)
    for first in range(0, rows, row_block):

        def count(c, total):
            row = lax.broadcasted_iota(jnp.int32, (row_block, chunk), 0) + first
            one = jnp.where(row == wide(2, c)[0:1, :], 1.0, 0.0).astype(BF16)
            return total + lax.dot_general(
                one, oh_dst[c, :, 0:chunk], contract_last, preferred_element_type=F32
            )

        total = lax.fori_loop(0, chunks, count, jnp.zeros((row_block, lon), F32))
        share = 1.0 / (1.0 + total)
        for r in range(row_block):
            inv_b[first + r] = jnp.broadcast_to(share[r : r + 1, :], inv_b.shape[1:])

    def transport(p):
        def substep(step, carry):
            for b in range(pband // 8):
                sub = slice(b * 8, (b + 1) * 8)
                at = slice(p * pband + b * 8, p * pband + (b + 1) * 8)
                north = speed[0, at, :] > 0
                east = speed[1, at, :] > 0
                zero = jnp.zeros((8, lon), F32)
                prior_flux, prior_diff = zero, None
                current = cells[p, 0, sub, :]
                ahead = cells[p, 1, sub, :]
                prior_diff = current
                flux, held = None, None

                def finish(i, value, below, flux, above):
                    t = i // spec
                    value = value - flux + jnp.where(north, below, above)
                    diff = pltpu.roll(value, lon - 1, 1) - value
                    slope = minmod(pltpu.roll(diff, 1, 1), diff)
                    g = coef[2, t, at, :] * value + coef[3, t, at, :] * slope
                    upwind = jnp.where(east, pltpu.roll(g, 1, 1), pltpu.roll(g, lon - 1, 1))
                    cells[p, i, sub, :] = (value - g + upwind) * mask_b[i]

                before, flux, held = zero, None, None
                for i in range(rows):
                    t = i // spec
                    diff = ahead - current
                    slope = minmod(prior_diff, diff)
                    g = coef[0, t, at, :] * current + coef[1, t, at, :] * slope
                    if i > 0:
                        finish(i - 1, held, before, flux, g)
                        before = flux
                    flux, held, prior_diff = g, current, diff
                    current = ahead
                    ahead = cells[p, i + 2, sub, :] if i + 2 < rows else zero
                finish(rows - 1, held, before, flux, zero)
            return carry

        lax.fori_loop(0, SUBSTEPS, substep, 0)

    def nest(p):
        def gather(c):
            x = cells[p, pl.ds(c * crows, crows)].reshape(crows * pband, lon)
            both = jnp.concatenate(split_high_low(x), axis=1)
            picked = jnp.dot(both, oh_src[c], preferred_element_type=F32)
            picked = picked.reshape(crows, pband, chunk)
            home = wide(0, c)[0:1, :] - c * crows
            total = jnp.where(home == 0, picked[0], 0.0)
            for r in range(1, crows):
                total = total + jnp.where(home == r, picked[r], 0.0)
            gathered[c] = total

        repeat(chunks, gather)
        for first in range(0, rows, row_block):

            def scatter(c, total):
                high, low = split_high_low(gathered[c])
                both = jnp.concatenate([high.astype(F32), low.astype(F32)], axis=1)
                home = wide(2, c)[0:1, :]
                home = jnp.concatenate([home, home], axis=1)
                left = [
                    jnp.where(home == first + r, both, 0.0) for r in range(row_block)
                ]
                left = jnp.concatenate(left, axis=0).astype(BF16)
                return total + lax.dot_general(
                    left, oh_dst[c], contract_last, preferred_element_type=F32
                )

            total = jnp.zeros((row_block * pband, lon), F32)
            if chunks <= 4:
                for c in range(chunks):
                    total = scatter(c, total)
            else:
                total = lax.fori_loop(0, chunks, scatter, total)
            total = total.reshape(row_block, pband, lon)
            for r in range(row_block):
                for b in range(pband // 8):
                    sub = slice(b * 8, (b + 1) * 8)
                    cells[p, first + r, sub, :] = (
                        cells[p, first + r, sub, :] + total[r, sub, :]
                    ) * inv_b[first + r]

    for p in range(parts):
        pltpu.make_async_copy(
            cells.at[p, pl.ds(0, n - 1)], cells.at[p, pl.ds(0, n - 1)], go_recv.at[p]
        ).wait()
        transport(p)
        nest(p)

        def send_back(k, c):
            q = peer(k)
            pltpu.make_async_remote_copy(
                src_ref=cells.at[p, q],
                dst_ref=inbox.at[me, p],
                send_sem=back_send.at[p],
                recv_sem=back_recv,
                device_id=target(q),
                device_id_type=MESH,
            ).start()
            return c

        lax.fori_loop(0, n - 1, send_back, 0)
        inbox[me, p] = cells[p, me]

    pltpu.make_async_copy(
        inbox.at[pl.ds(0, n - 1)], inbox.at[pl.ds(0, n - 1)], back_recv
    ).wait()
    if band % 8 == 0:
        merged = inbox[...].reshape(bins, lon)
    else:
        for q in range(n):
            field[q * band : (q + 1) * band, :] = inbox[q, 0, 0:band, :]
        merged = field[...]
    out[...] = source(merged) * own_mask

    pltpu.make_async_copy(
        meta.at[pl.ds(0, tiles - 1)], meta.at[pl.ds(0, tiles - 1)], meta_send
    ).wait()
    for p in range(parts):
        sent = outbox.at[pl.ds(0, n - 1), p]
        pltpu.make_async_copy(sent, sent, go_send.at[p]).wait()
        sent = cells.at[p, pl.ds(0, n - 1)]
        pltpu.make_async_copy(sent, sent, back_send.at[p]).wait()


def shards(
    spectra,
    quad_first,
    quad_second,
    quad_output,
    owner_map,
    land_mask,
    nest_dest,
    nest_src,
    nest_into,
):
    spec = lax.axis_size("spec")
    tiles = lax.axis_size("space")
    n = spec * tiles
    bins, _, lon = spectra.shape
    band = bins // n
    parts = PARTS if band % (8 * PARTS) == 0 else 1
    pband = band // parts if band % 8 == 0 else -(-band // 8) * 8
    entries = nest_dest.shape[0]
    width = min(entries, lon)
    erows = entries // width
    meta_rows = -(-(-(-spec // 8) * 8 + 3 * erows) // 8) * 8
    total = tiles * entries
    chunk = max(entries, min(2 * lon, total))
    chunks = total // chunk
    dims = (n, tiles, spec, bins, lon, band, parts, pband, entries)
    vmem = pl.BlockSpec(memory_space=pltpu.VMEM)
    hbm = pl.BlockSpec(memory_space=pl.ANY)
    V = pltpu.VMEM
    dma = pltpu.SemaphoreType.DMA
    result = pl.pallas_call(
        functools.partial(kernel, dims),
        out_shape=jax.ShapeDtypeStruct((bins, lon), F32),
        in_specs=[hbm] * 4 + [pl.BlockSpec(memory_space=pltpu.SMEM)] + [vmem] * 4,
        out_specs=vmem,
        scratch_shapes=[
            V((bins, lon), F32),
            V(quad_first.shape, BF16),
            V(quad_second.shape, BF16),
            V(quad_output.shape, BF16),
            V((n, parts, pband, lon), F32),
            V((parts, n, pband, lon), F32),
            V((n, parts, pband, lon), F32),
            V((tiles, meta_rows, lon), jnp.int32),
            V((4, total // lon, 8, lon), jnp.int32),
            V((n, 8, lon), F32),
            V((n, 8, lon), F32),
            V((4, tiles, parts * pband, lon), F32),
            V((2, parts * pband, lon), F32),
            V((chunks, 2 * lon, chunk), BF16),
            V((chunks, lon, 2 * chunk), BF16),
            V((chunks, pband, chunk), F32),
            dma((4,)),
            dma,
            dma,
            dma((parts,)),
            dma((parts,)),
            dma((parts,)),
            dma,
        ],
        compiler_params=pltpu.CompilerParams(
            collective_id=0, has_side_effects=True, vmem_limit_bytes=48 * 1024 * 1024
        ),
        cost_estimate=pl.CostEstimate(
            flops=12 * bins * bins * lon, bytes_accessed=6 * bins * bins + 8 * bins * lon, transcendentals=0
        ),
    )(
        spectra.reshape(bins, lon),
        quad_first,
        quad_second,
        quad_output,
        owner_map,
        land_mask,
        nest_dest.reshape(erows, width),
        nest_src.reshape(erows, width),
        nest_into.reshape(erows, width),
    )
    return result.reshape(spectra.shape)


def solution(mesh):
    return jax.shard_map(
        shards,
        mesh=mesh,
        in_specs=(
            P(None, ("space", "spec"), None),
            P(),
            P(),
            P(),
            P(),
            P("space", None),
            P("space"),
            P("space"),
            P("space"),
        ),
        out_specs=P(None, ("space", "spec"), None),
        check_vma=False,
    )
```

time: 164 us -> 75.3 us (0.46)
  Pallas kernels: 0 us -> 66.1 us
  starting transfers between devices: 53.9 us -> 0 us
  waiting for transfers between devices: 48.2 us -> 0 us
  other arithmetic: 25.5 us -> 0 us
  blocking collectives: 10.9 us -> 0 us
  matrix products: 8.53 us -> 0 us
  local copies, waits for them, and re-layouts: 15.4 us -> 8.85 us
    pallas_call x0 -> x1, Pallas kernels: none -> 66.1 us  [shards(): pl.pallas_call(functools.partial(kernel, dims), out_shape=jax.ShapeDtypeS...]
    ppermute x12 -> x0, waiting for transfers between devices: 35.5 us -> none  [the longest x6 27 us: padded_2(): after = lax.ppermute(leading, axis, down)]
    ppermute x12 -> x0, starting transfers between devices: 34.3 us -> none  [the longest x6 26.1 us: padded_2(): before = lax.ppermute(last, axis, up)]
    all_to_all x3 -> x0, starting transfers between devices: 19.6 us -> none  [the longest x1 8.16 us: shards(): lax.all_to_all(targets, 'space', split_axis=1, concat_axis=1, tiled=True)]
    all_to_all x3 -> x0, waiting for transfers between devices: 12.7 us -> none  [the longest x1 6.8 us: shards(): lax.all_to_all(sourced, 'spec', split_axis=0, concat_axis=1, tiled=True)]
    all_to_all x1 -> x0, blocking collectives: 10.9 us -> none  [shards(): lax.all_to_all(merged.reshape(band_bins, spec_count, lon_cols), 'spec', s...]
    select_n x16 -> x0, other arithmetic: 9.36 us -> none  [the longest x12 9.33 us: upwind_sweep(): jnp.where(forward, lax.slice_in_dim(upper_flux, 0, face_count, axis=axis_...]
    dot_general x4 -> x0, matrix products: 8.53 us -> none  [the longest x2 5.09 us: source_update(): lax.dot_general(quad_output, product, contract, preferred_element_type=jn...]
  transfers between devices with their start and end apart: 15 -> 0, of which waited for: 12 -> 0; matrix products, arithmetic and copies ran while one was open for 8% -> 0% of each run, Pallas kernels for 0% -> 0%
where the time goes in v1:
time: 75.3 us; the launch traced here: 75 us
  Pallas kernels  66.1 us (88%)
  local copies, waits for them, and re-layouts  8.85 us (12%)
    pallas_call x1, Pallas kernels, shards(): pl.pallas_call(functools.partial(kernel, dims), out_shape=jax.ShapeDtypeS...  66.1 us
    unnamed x19, local copies, waits for them, and re-layouts  8.85 us

profile of v1, /device:TPU:0, one launch (start us, length us, event | category | flops | bytes accessed | tf_op | source)
XLA Modules:
  0.0 75.0 jit_solution(1896390913421588208)
XLA Ops:
  0.0 0.0 copy-start
  0.0 1.3 %copy-done = bf16[768,768]{1,0:T(8,128)(2,1)S(1)} copy-done((bf16[768,768]{1,0:T(8,128)(2,1)S(1)}, bf16[768,768]{1,0:T(8,128)(2,1)}, u32[]{:S(2)}) %copy-start) | copy-done | bytes 1179672
  1.3 0.0 copy-start.1
  1.3 1.3 %copy-done.1 = bf16[768,768]{1,0:T(8,128)(2,1)S(1)} copy-done((bf16[768,768]{1,0:T(8,128)(2,1)S(1)}, bf16[768,768]{1,0:T(8,128)(2,1)}, u32[]{:S(2)}) %copy-start.1) | copy-done | bytes 1179672
  2.5 0.0 copy-start.2
  2.5 1.3 %copy-done.2 = bf16[768,768]{1,0:T(8,128)(2,1)S(1)} copy-done((bf16[768,768]{1,0:T(8,128)(2,1)S(1)}, bf16[768,768]{1,0:T(8,128)(2,1)}, u32[]{:S(2)}) %copy-start.2) | copy-done | bytes 1179672
  3.8 0.0 copy-start.3
  3.8 1.0 %copy-done.3 = f32[768,1,128]{2,1,0:T(1,128)S(1)} copy-done((f32[768,1,128]{2,1,0:T(1,128)S(1)}, f32[768,1,128]{2,1,0:T(1,128)}, u32[]{:S(2)}) %copy-start.3) | copy-done | bytes 393240
  4.8 0.0 copy-start.4
  4.8 0.7 copy-done.4
  5.5 0.0 copy-start.5
  5.5 0.7 copy-done.5
  6.1 0.0 copy-start.6
  6.2 0.7 copy-done.6
  6.8 0.0 copy-start.7
  6.8 0.7 copy-done.7
  7.5 0.0 copy-start.8
  7.5 0.7 copy-done.8
  8.1 66.1 %shard_map.91 = f32[768,128]{1,0:T(8,128)S(1)} custom-call(f32[768,128]{1,0:T(8,128)S(1)} %bitcast.8, bf16[768,768]{1,0:T(8,128)(2,1)S(1)} %copy-done, bf16[768,768]{1,0:T(8,128)(2,1)S(1)} %copy-done.1, bf16[768,768]{1,0:T(8,128)(2,1)S(1)} %copy-done.2, s32[8]{0:T(128)S(1)} %copy-done.5, s32[4,128]{1,0:T(4,128)S(1)} %copy-done.4, s32[1,64]{1,0:T(1,128)S(1)} %bitcast.9, ...), custom_call_target="tpu_custom_call" | custom-call | flops 905969664 | bytes 4325376 | tf_op jit(solution)/shard_map/pallas_call | solution.py:382
  74.3 0.7 copy.12
Async XLA Ops:
  0.0 1.3 %copy-start = (bf16[768,768]{1,0:T(8,128)(2,1)S(1)}, bf16[768,768]{1,0:T(8,128)(2,1)}, u32[]{:S(2)}) copy-start(bf16[768,768]{1,0:T(8,128)(2,1)} %quad_first.1) | copy-start | bytes 3538948
  1.3 1.3 %copy-start.1 = (bf16[768,768]{1,0:T(8,128)(2,1)S(1)}, bf16[768,768]{1,0:T(8,128)(2,1)}, u32[]{:S(2)}) copy-start(bf16[768,768]{1,0:T(8,128)(2,1)} %quad_second.1) | copy-start | bytes 3538948
  2.5 1.3 %copy-start.2 = (bf16[768,768]{1,0:T(8,128)(2,1)S(1)}, bf16[768,768]{1,0:T(8,128)(2,1)}, u32[]{:S(2)}) copy-start(bf16[768,768]{1,0:T(8,128)(2,1)} %quad_output.1) | copy-start | bytes 3538948
  3.8 1.0 %copy-start.3 = (f32[768,1,128]{2,1,0:T(1,128)S(1)}, f32[768,1,128]{2,1,0:T(1,128)}, u32[]{:S(2)}) copy-start(f32[768,1,128]{2,1,0:T(1,128)} %param.9) | copy-start | bytes 1179652
  4.8 0.7 copy-start.4
  5.5 0.7 copy-start.5
  6.1 0.7 copy-start.6
  6.8 0.7 copy-start.7
  7.5 0.7 copy-start.8

commit v2 on v1

--- a/solution.py
+++ b/solution.py
@@ -11,7 +11,7 @@
 DIRS = 24
 SUBSTEPS = 6
 FREQS = 32
-PARTS = 1
+PARTS = 3
 
 step_weight = 0.25
 grid_factors = (1.0, 0.55, 0.3)
@@ -40,9 +40,9 @@
 
 def kernel(
     dims,
-    spectra, quad_first, quad_second, quad_output, owner, land, dest, src, into,
+    spectra, quad_first, quad_second, quad_output, owner_in, land_in, dest_in, src_in, into_in,
     out,
-    field, w1, w2, w3, outbox, cells, inbox, meta, ent, mask_b, inv_b, coef, speed, oh_src, oh_dst, gathered,
+    owner, land, dest, src, into, field, w1, w2, w3, outbox, cells, inbox, meta, ent, mask_b, inv_b, coef, speed, oh_src, oh_dst, gathered,
     load_sem, meta_send, meta_recv, go_send, go_recv, back_send, back_recv,
 ):
     n, tiles, spec, bins, lon, band, parts, pband, entries = dims
@@ -55,40 +55,51 @@
     loads = [
         pltpu.make_async_copy(a, b, load_sem.at[i])
         for i, (a, b) in enumerate(
-            ((spectra, field), (quad_first, w1), (quad_second, w2), (quad_output, w3))
+            (
+                (land_in, land), (dest_in, dest), (src_in, src), (into_in, into), (owner_in, owner),
+                (spectra, field), (quad_first, w1), (quad_second, w2), (quad_output, w3),
+            )
         )
     ]
     for copy in loads:
         copy.start()
 
-    def target(q):
-        return {"space": lax.div(q, spec), "spec": lax.rem(q, spec)}
-
-    def peer(k):
-        half = lax.div(k + 1, 2)
-        offset = n // 2 + half * (1 - 2 * lax.rem(k, 2))
-        return lax.rem(me + offset, n)
+    def peers(visit):
+        def one_tile(j, c):
+            offset = tiles // 2 + lax.div(j + 1, 2) * (1 - 2 * lax.rem(j, 2))
+            t = tile + offset
+            t = jnp.where(t >= tiles, t - tiles, t)
+            for k in range(spec):
+                r = spec_rank + k
+                visit(t, jnp.where(r >= spec, r - spec, r))
+            return c
+
+        lax.fori_loop(0, tiles - 1, one_tile, 0)
+        for k in range(1, spec):
+            r = spec_rank + k
+            visit(tile, jnp.where(r >= spec, r - spec, r))
 
     barrier = pltpu.get_barrier_semaphore()
 
-    def greet(k, c):
-        pl.semaphore_signal(barrier, inc=1, device_id=target(peer(k)), device_id_type=MESH)
-        return c
-
-    lax.fori_loop(0, n - 1, greet, 0)
+    def greet(t, r):
+        pl.semaphore_signal(
+            barrier, inc=1, device_id={"space": t, "spec": r}, device_id_type=MESH
+        )
+
+    peers(greet)
 
     width = min(entries, lon)
     per = lon // width
     erows = entries // width
     base = -(-spec // 8) * 8
+    for copy in loads[:5]:
+        copy.wait()
     mine = jnp.zeros(meta.shape[1:], jnp.int32)
     meta[tile] = mine
     meta[tile, 0:spec, :] = land[...]
     for j, part in enumerate((dest, src, into)):
         meta[tile, base + j * erows : base + (j + 1) * erows, 0:width] = part[...]
     own_mask = land[pl.ds(spec_rank, 1), :].astype(F32)
-
-    pl.semaphore_wait(barrier, n - 1)
 
     def meta_copy(k):
         return pltpu.make_async_remote_copy(
@@ -104,8 +115,6 @@
         meta_copy(k).start()
         return c
 
-    lax.fori_loop(1, tiles, send_meta, 0)
-
     def source(x):
         xt = x.T.astype(BF16)
         one = jnp.dot(xt, w1[...], preferred_element_type=F32)
@@ -114,7 +123,7 @@
         tendency = jnp.dot(product, w3[...], preferred_element_type=F32)
         return x + step_weight * tendency.T
 
-    for copy in loads:
+    for copy in loads[5:]:
         copy.wait()
     sourced = source(field[...]) * own_mask
     if band % 8 == 0:
@@ -125,24 +134,28 @@
         for q in range(n):
             outbox[q, 0, 0:band, :] = field[q * band : (q + 1) * band, :]
 
-    for p in range(parts):
-
-        def send(k, c):
-            q = peer(k)
+    pl.semaphore_wait(barrier, n - 1)
+    lax.fori_loop(1, tiles, send_meta, 0)
+
+    def send_part(p, c):
+        def send(t, r):
             pltpu.make_async_remote_copy(
-                src_ref=outbox.at[q, p],
+                src_ref=outbox.at[t * spec + r, p],
                 dst_ref=cells.at[p, me],
                 send_sem=go_send.at[p],
                 recv_sem=go_recv.at[p],
-                device_id=target(q),
+                device_id={"space": t, "spec": r},
                 device_id_type=MESH,
             ).start()
-            return c
-
-        lax.fori_loop(0, n - 1, send, 0)
+
+        peers(send)
         cells[p, me] = outbox[me, p]
-
-    local = lax.broadcasted_iota(jnp.int32, (parts * pband, lon), 0)
+        return c
+
+    lax.fori_loop(0, parts, send_part, 0)
+
+    local = lax.broadcasted_iota(jnp.int32, (parts, pband, lon), 1)
+    local = local + lax.broadcasted_iota(jnp.int32, (parts, pband, lon), 0) * pband
     index = (local + me * band).astype(F32)
     freq = jnp.floor((index + 0.5) * (1.0 / DIRS))
     direction = (index - DIRS * freq + 0.5) * (2.0 * math.pi / DIRS)
@@ -228,22 +241,19 @@
         def substep(step, carry):
             for b in range(pband // 8):
                 sub = slice(b * 8, (b + 1) * 8)
-                at = slice(p * pband + b * 8, p * pband + (b + 1) * 8)
-                north = speed[0, at, :] > 0
-                east = speed[1, at, :] > 0
+                north = speed[0, p, sub, :] > 0
+                east = speed[1, p, sub, :] > 0
                 zero = jnp.zeros((8, lon), F32)
-                prior_flux, prior_diff = zero, None
                 current = cells[p, 0, sub, :]
                 ahead = cells[p, 1, sub, :]
                 prior_diff = current
-                flux, held = None, None
 
                 def finish(i, value, below, flux, above):
                     t = i // spec
                     value = value - flux + jnp.where(north, below, above)
                     diff = pltpu.roll(value, lon - 1, 1) - value
                     slope = minmod(pltpu.roll(diff, 1, 1), diff)
-                    g = coef[2, t, at, :] * value + coef[3, t, at, :] * slope
+                    g = coef[2, t, p, sub, :] * value + coef[3, t, p, sub, :] * slope
                     upwind = jnp.where(east, pltpu.roll(g, 1, 1), pltpu.roll(g, lon - 1, 1))
                     cells[p, i, sub, :] = (value - g + upwind) * mask_b[i]
 
@@ -252,7 +262,7 @@
                     t = i // spec
                     diff = ahead - current
                     slope = minmod(prior_diff, diff)
-                    g = coef[0, t, at, :] * current + coef[1, t, at, :] * slope
+                    g = coef[0, t, p, sub, :] * current + coef[1, t, p, sub, :] * slope
                     if i > 0:
                         finish(i - 1, held, before, flux, g)
                         before = flux
@@ -306,27 +316,28 @@
                         cells[p, first + r, sub, :] + total[r, sub, :]
                     ) * inv_b[first + r]
 
-    for p in range(parts):
+    def one_part(p, c):
         pltpu.make_async_copy(
             cells.at[p, pl.ds(0, n - 1)], cells.at[p, pl.ds(0, n - 1)], go_recv.at[p]
         ).wait()
         transport(p)
         nest(p)
 
-        def send_back(k, c):
-            q = peer(k)
+        def send_back(t, r):
             pltpu.make_async_remote_copy(
-                src_ref=cells.at[p, q],
+                src_ref=cells.at[p, t * spec + r],
                 dst_ref=inbox.at[me, p],
                 send_sem=back_send.at[p],
                 recv_sem=back_recv,
-                device_id=target(q),
+                device_id={"space": t, "spec": r},
                 device_id_type=MESH,
             ).start()
-            return c
-
-        lax.fori_loop(0, n - 1, send_back, 0)
+
+        peers(send_back)
         inbox[me, p] = cells[p, me]
+        return c
+
+    lax.fori_loop(0, parts, one_part, 0)
 
     pltpu.make_async_copy(
         inbox.at[pl.ds(0, n - 1)], inbox.at[pl.ds(0, n - 1)], back_recv
@@ -376,15 +387,20 @@
     chunks = total // chunk
     dims = (n, tiles, spec, bins, lon, band, parts, pband, entries)
     vmem = pl.BlockSpec(memory_space=pltpu.VMEM)
-    hbm = pl.BlockSpec(memory_space=pl.ANY)
+    hbm = pl.BlockSpec(memory_space=pltpu.HBM)
     V = pltpu.VMEM
     dma = pltpu.SemaphoreType.DMA
     result = pl.pallas_call(
         functools.partial(kernel, dims),
         out_shape=jax.ShapeDtypeStruct((bins, lon), F32),
-        in_specs=[hbm] * 4 + [pl.BlockSpec(memory_space=pltpu.SMEM)] + [vmem] * 4,
+        in_specs=[hbm] * 9,
         out_specs=vmem,
         scratch_shapes=[
+            pltpu.SMEM(owner_map.shape, jnp.int32),
+            V(land_mask.shape, jnp.int32),
+            V((erows, width), jnp.int32),
+            V((erows, width), jnp.int32),
+            V((erows, width), jnp.int32),
             V((bins, lon), F32),
             V(quad_first.shape, BF16),
             V(quad_second.shape, BF16),
@@ -396,12 +412,12 @@
             V((4, total // lon, 8, lon), jnp.int32),
             V((n, 8, lon), F32),
             V((n, 8, lon), F32),
-            V((4, tiles, parts * pband, lon), F32),
-            V((2, parts * pband, lon), F32),
+            V((4, tiles, parts, pband, lon), F32),
+            V((2, parts, pband, lon), F32),
             V((chunks, 2 * lon, chunk), BF16),
             V((chunks, lon, 2 * chunk), BF16),
             V((chunks, pband, chunk), F32),
-            dma((4,)),
+            dma((9,)),
             dma,
             dma,
             dma((parts,)),
@@ -410,7 +426,7 @@
             dma,
         ],
         compiler_params=pltpu.CompilerParams(
-            collective_id=0, has_side_effects=True, vmem_limit_bytes=48 * 1024 * 1024
+            collective_id=0, has_side_effects=True, vmem_limit_bytes=56 * 1024 * 1024
         ),
         cost_estimate=pl.CostEstimate(
             flops=12 * bins * bins * lon, bytes_accessed=6 * bins * bins + 8 * bins * lon, transcendentals=0

time: 75.3 us -> 32.6 us (0.43)
  Pallas kernels: 66.1 us -> 30.7 us
  local copies, waits for them, and re-layouts: 8.85 us -> 1.77 us
    pallas_call x1, Pallas kernels: 66.1 us -> 30.7 us  [shards(): pl.pallas_call(functools.partial(kernel, dims), out_shape=jax.ShapeDtypeS...]
    unnamed x19 -> x1, local copies, waits for them, and re-layouts: 8.85 us -> 1.77 us
where the time goes in v2:
time: 32.6 us; the launch traced here: 32.5 us
  Pallas kernels  30.7 us (94%)
  local copies, waits for them, and re-layouts  1.77 us (5%)
    pallas_call x1, Pallas kernels, shards(): pl.pallas_call(functools.partial(kernel, dims), out_shape=jax.ShapeDtypeS...  30.7 us
    unnamed x1, local copies, waits for them, and re-layouts  1.77 us

profile of v2, /device:TPU:0, one launch (start us, length us, event | category | flops | bytes accessed | tf_op | source)
XLA Modules:
  0.0 32.5 jit_solution(4465556782346350919)
XLA Ops:
  0.0 30.7 %shard_map.91 = f32[768,128]{1,0:T(8,128)} custom-call(f32[768,128]{1,0:T(8,128)} %bitcast.8, bf16[768,768]{1,0:T(8,128)(2,1)} %quad_first.1, bf16[768,768]{1,0:T(8,128)(2,1)} %quad_second.1, bf16[768,768]{1,0:T(8,128)(2,1)} %quad_output.1, s32[8]{0:T(128)} %owner_in.1, s32[4,128]{1,0:T(4,128)} %land_in.1, s32[1,64]{1,0:T(1,128)} %bitcast.9, ...), custom_call_target="tpu_custom_call" | custom-call | flops 905969664 | bytes 4325376 | tf_op jit(solution)/shard_map/pallas_call | solution.py:393
  30.7 1.8 %copy.12 = f32[768,1,128]{2,1,0:T(1,128)} copy(f32[768,1,128]{2,1,0:T(1,128)} %bitcast.7) | data formatting | bytes 786432

commit v3 on v2

--- a/solution.py
+++ b/solution.py
@@ -41,8 +41,8 @@
 def kernel(
     dims,
     spectra, quad_first, quad_second, quad_output, owner_in, land_in, dest_in, src_in, into_in,
-    out,
-    owner, land, dest, src, into, field, w1, w2, w3, outbox, cells, inbox, meta, ent, mask_b, inv_b, coef, speed, oh_src, oh_dst, gathered,
+    out, out_mask,
+    owner, land, dest, src, into, field, w1, w2, w3, outbox, cells, inbox, sums, meta, ent, mask_b, inv_b, coef, speed, oh_src, oh_dst, gathered,
     load_sem, meta_send, meta_recv, go_send, go_recv, back_send, back_recv,
 ):
     n, tiles, spec, bins, lon, band, parts, pband, entries = dims
@@ -115,32 +115,14 @@
         meta_copy(k).start()
         return c
 
-    def source(x):
-        xt = x.T.astype(BF16)
-        one = jnp.dot(xt, w1[...], preferred_element_type=F32)
-        two = jnp.dot(xt, w2[...], preferred_element_type=F32)
-        product = (one * two).astype(BF16)
-        tendency = jnp.dot(product, w3[...], preferred_element_type=F32)
-        return x + step_weight * tendency.T
-
-    for copy in loads[5:]:
-        copy.wait()
-    sourced = source(field[...]) * own_mask
-    if band % 8 == 0:
-        outbox[...] = sourced.reshape(n, parts, pband, lon)
-    else:
-        field[...] = sourced
-        outbox[...] = jnp.zeros_like(outbox)
-        for q in range(n):
-            outbox[q, 0, 0:band, :] = field[q * band : (q + 1) * band, :]
-
-    pl.semaphore_wait(barrier, n - 1)
-    lax.fori_loop(1, tiles, send_meta, 0)
-
-    def send_part(p, c):
+    def third(product, p):
+        columns = slice(p * width_p, (p + 1) * width_p)
+        return step_weight * jnp.dot(product, w3[:, columns], preferred_element_type=F32).T
+
+    def send_part(p):
         def send(t, r):
             pltpu.make_async_remote_copy(
-                src_ref=outbox.at[t * spec + r, p],
+                src_ref=outbox.at[p, t * spec + r],
                 dst_ref=cells.at[p, me],
                 send_sem=go_send.at[p],
                 recv_sem=go_recv.at[p],
@@ -149,14 +131,33 @@
             ).start()
 
         peers(send)
-        cells[p, me] = outbox[me, p]
-        return c
-
-    lax.fori_loop(0, parts, send_part, 0)
+        cells[p, me] = outbox[p, me]
+
+    width_p = bins // parts
+    loads[5].wait()
+    turned = field[...].T.astype(BF16)
+    loads[6].wait()
+    one = jnp.dot(turned, w1[...], preferred_element_type=F32)
+    loads[7].wait()
+    two = jnp.dot(turned, w2[...], preferred_element_type=F32)
+    product = (one * two).astype(BF16)
+    loads[8].wait()
+    pl.semaphore_wait(barrier, n - 1)
+    lax.fori_loop(1, tiles, send_meta, 0)
+    for p in range(parts):
+        sourced = (field[p * width_p : (p + 1) * width_p, :] + third(product, p)) * own_mask
+        if band % 8 == 0:
+            outbox[p] = sourced.reshape(n, pband, lon)
+        else:
+            field[...] = sourced
+            outbox[...] = jnp.zeros_like(outbox)
+            for q in range(n):
+                outbox[0, q, 0:band, :] = field[q * band : (q + 1) * band, :]
+        send_part(p)
 
     local = lax.broadcasted_iota(jnp.int32, (parts, pband, lon), 1)
-    local = local + lax.broadcasted_iota(jnp.int32, (parts, pband, lon), 0) * pband
-    index = (local + me * band).astype(F32)
+    local = local + lax.broadcasted_iota(jnp.int32, (parts, pband, lon), 0) * width_p
+    index = (local + me * (band // parts)).astype(F32)
     freq = jnp.floor((index + 0.5) * (1.0 / DIRS))
     direction = (index - DIRS * freq + 0.5) * (2.0 * math.pi / DIRS)
     speeds = 0.2 + 0.7 * (freq + 0.5) / FREQS
@@ -326,35 +327,48 @@
         def send_back(t, r):
             pltpu.make_async_remote_copy(
                 src_ref=cells.at[p, t * spec + r],
-                dst_ref=inbox.at[me, p],
+                dst_ref=inbox.at[p, me],
                 send_sem=back_send.at[p],
-                recv_sem=back_recv,
+                recv_sem=back_recv.at[p],
                 device_id={"space": t, "spec": r},
                 device_id_type=MESH,
             ).start()
 
         peers(send_back)
-        inbox[me, p] = cells[p, me]
+        inbox[p, me] = cells[p, me]
         return c
 
     lax.fori_loop(0, parts, one_part, 0)
 
-    pltpu.make_async_copy(
-        inbox.at[pl.ds(0, n - 1)], inbox.at[pl.ds(0, n - 1)], back_recv
-    ).wait()
-    if band % 8 == 0:
-        merged = inbox[...].reshape(bins, lon)
-    else:
-        for q in range(n):
-            field[q * band : (q + 1) * band, :] = inbox[q, 0, 0:band, :]
-        merged = field[...]
-    out[...] = source(merged) * own_mask
+    for p in range(parts):
+        arrived = inbox.at[p, pl.ds(0, n - 1)]
+        pltpu.make_async_copy(arrived, arrived, back_recv.at[p]).wait()
+        rows_p = slice(p * width_p, (p + 1) * width_p)
+        if band % 8 == 0:
+            field[rows_p, :] = inbox[p].reshape(width_p, lon)
+        else:
+            for q in range(n):
+                field[q * band : (q + 1) * band, :] = inbox[0, q, 0:band, :]
+        turned = field[rows_p, :].T.astype(BF16)
+        one = jnp.dot(turned, w1[rows_p, :], preferred_element_type=F32)
+        two = jnp.dot(turned, w2[rows_p, :], preferred_element_type=F32)
+        if p > 0:
+            one = one + sums[0]
+            two = two + sums[1]
+        if p < parts - 1:
+            sums[0] = one
+            sums[1] = two
+    product = (one * two).astype(BF16)
+    for p in range(parts):
+        rows_p = slice(p * width_p, (p + 1) * width_p)
+        out[rows_p, :] = field[rows_p, :] + third(product, p)
+    out_mask[...] = own_mask
 
     pltpu.make_async_copy(
         meta.at[pl.ds(0, tiles - 1)], meta.at[pl.ds(0, tiles - 1)], meta_send
     ).wait()
     for p in range(parts):
-        sent = outbox.at[pl.ds(0, n - 1), p]
+        sent = outbox.at[p, pl.ds(0, n - 1)]
         pltpu.make_async_copy(sent, sent, go_send.at[p]).wait()
         sent = cells.at[p, pl.ds(0, n - 1)]
         pltpu.make_async_copy(sent, sent, back_send.at[p]).wait()
@@ -390,11 +404,11 @@
     hbm = pl.BlockSpec(memory_space=pltpu.HBM)
     V = pltpu.VMEM
     dma = pltpu.SemaphoreType.DMA
-    result = pl.pallas_call(
+    result, own_row = pl.pallas_call(
         functools.partial(kernel, dims),
-        out_shape=jax.ShapeDtypeStruct((bins, lon), F32),
+        out_shape=[jax.ShapeDtypeStruct((bins, lon), F32), jax.ShapeDtypeStruct((1, lon), F32)],
         in_specs=[hbm] * 9,
-        out_specs=vmem,
+        out_specs=[vmem, vmem],
         scratch_shapes=[
             pltpu.SMEM(owner_map.shape, jnp.int32),
             V(land_mask.shape, jnp.int32),
@@ -405,9 +419,10 @@
             V(quad_first.shape, BF16),
             V(quad_second.shape, BF16),
             V(quad_output.shape, BF16),
-            V((n, parts, pband, lon), F32),
             V((parts, n, pband, lon), F32),
-            V((n, parts, pband, lon), F32),
+            V((parts, n, pband, lon), F32),
+            V((parts, n, pband, lon), F32),
+            V((2, lon, bins), F32),
             V((tiles, meta_rows, lon), jnp.int32),
             V((4, total // lon, 8, lon), jnp.int32),
             V((n, 8, lon), F32),
@@ -423,7 +438,7 @@
             dma((parts,)),
             dma((parts,)),
             dma((parts,)),
-            dma,
+            dma((parts,)),
         ],
         compiler_params=pltpu.CompilerParams(
             collective_id=0, has_side_effects=True, vmem_limit_bytes=56 * 1024 * 1024
@@ -442,7 +457,7 @@
         nest_src.reshape(erows, width),
         nest_into.reshape(erows, width),
     )
-    return result.reshape(spectra.shape)
+    return (result * own_row).reshape(spectra.shape)
 
 
 def solution(mesh):

time: 32.6 us -> 32.4 us (level)
  other arithmetic: 0 us -> 1.77 us
  local copies, waits for them, and re-layouts: 1.77 us -> 0 us
    mul x0 -> x1, other arithmetic: none -> 1.77 us  [shards(): return (result * own_row).reshape(spectra.shape)]
    unnamed x1 -> x0, local copies, waits for them, and re-layouts: 1.77 us -> none
where the time goes in v3:
time: 32.4 us; the launch traced here: 32.3 us
  Pallas kernels  30.5 us (94%)
  other arithmetic  1.77 us (5%)
    pallas_call x1, Pallas kernels, shards(): pl.pallas_call(functools.partial(kernel, dims), out_shape=[jax.ShapeDtype...  30.5 us
    mul x1, other arithmetic, shards(): return (result * own_row).reshape(spectra.shape)  1.77 us

profile of v3, /device:TPU:0, one launch (start us, length us, event | category | flops | bytes accessed | tf_op | source)
XLA Modules:
  0.0 32.3 jit_solution(12555684397605854126)
XLA Ops:
  0.0 30.5 %shard_map.91 = (f32[768,128]{1,0:T(8,128)}, f32[1,128]{1,0:T(1,128)}) custom-call(f32[768,128]{1,0:T(8,128)} %bitcast.8, bf16[768,768]{1,0:T(8,128)(2,1)} %quad_first.1, bf16[768,768]{1,0:T(8,128)(2,1)} %quad_second.1, bf16[768,768]{1,0:T(8,128)(2,1)} %quad_output.1, s32[8]{0:T(128)} %owner_in.1, s32[4,128]{1,0:T(4,128)} %land_in.1, s32[1,64]{1,0:T(1,128)} %bitcast.9, ...), custom_call_target="tpu_custom_call" | custom-call | flops 905969664 | bytes 4325376 | tf_op jit(solution)/shard_map/pallas_call | solution.py:407
  30.5 1.8 %broadcast_multiply_fusion = f32[768,128]{1,0:T(8,128)} fusion(f32[768,128]{1,0:T(8,128)} %get-tuple-element.7, f32[128]{0:T(128)} %bitcast.12), kind=kLoop, calls=%fused_computation | loop fusion | flops 98304 | bytes 786944 | tf_op jit(solution)/shard_map/mul | solution.py:460

commit v4 on v3

--- a/solution.py
+++ b/solution.py
@@ -134,6 +134,24 @@
         cells[p, me] = outbox[p, me]
 
     width_p = bins // parts
+    local = lax.broadcasted_iota(jnp.int32, (parts, pband, lon), 1)
+    local = local + lax.broadcasted_iota(jnp.int32, (parts, pband, lon), 0) * width_p
+    index = (local + me * (band // parts)).astype(F32)
+    freq = jnp.floor((index + 0.5) * (1.0 / DIRS))
+    direction = (index - DIRS * freq + 0.5) * (2.0 * math.pi / DIRS)
+    speeds = 0.2 + 0.7 * (freq + 0.5) / FREQS
+    speed[0] = speeds * jnp.cos(direction)
+    speed[1] = speeds * jnp.sin(direction)
+    for t in range(tiles):
+        grid = owner[t]
+        factor = jnp.where(
+            grid == 0, grid_factors[0], jnp.where(grid == 1, grid_factors[1], grid_factors[2])
+        ).astype(F32)
+        for axis in range(2):
+            courant = speed[axis] * factor
+            coef[2 * axis, t] = jnp.abs(courant)
+            coef[2 * axis + 1, t] = 0.5 * courant * (1.0 - jnp.abs(courant))
+
     loads[5].wait()
     turned = field[...].T.astype(BF16)
     loads[6].wait()
@@ -154,24 +172,6 @@
             for q in range(n):
                 outbox[0, q, 0:band, :] = field[q * band : (q + 1) * band, :]
         send_part(p)
-
-    local = lax.broadcasted_iota(jnp.int32, (parts, pband, lon), 1)
-    local = local + lax.broadcasted_iota(jnp.int32, (parts, pband, lon), 0) * width_p
-    index = (local + me * (band // parts)).astype(F32)
-    freq = jnp.floor((index + 0.5) * (1.0 / DIRS))
-    direction = (index - DIRS * freq + 0.5) * (2.0 * math.pi / DIRS)
-    speeds = 0.2 + 0.7 * (freq + 0.5) / FREQS
-    speed[0] = speeds * jnp.cos(direction)
-    speed[1] = speeds * jnp.sin(direction)
-    for t in range(tiles):
-        grid = owner[t]
-        factor = jnp.where(
-            grid == 0, grid_factors[0], jnp.where(grid == 1, grid_factors[1], grid_factors[2])
-        ).astype(F32)
-        for axis in range(2):
-            courant = speed[axis] * factor
-            coef[2 * axis, t] = jnp.abs(courant)
-            coef[2 * axis + 1, t] = 0.5 * courant * (1.0 - jnp.abs(courant))
 
     drained = pltpu.make_async_copy(
         meta.at[pl.ds(0, tiles - 1)], meta.at[pl.ds(0, tiles - 1)], meta_recv
@@ -238,42 +238,54 @@
         for r in range(row_block):
             inv_b[first + r] = jnp.broadcast_to(share[r : r + 1, :], inv_b.shape[1:])
 
+    def substep(p, sub, values):
+        north = speed[0, p, sub, :] > 0
+        east = speed[1, p, sub, :] > 0
+        zero = jnp.zeros((8, lon), F32)
+
+        def along_row(i, value, flux, below, above):
+            t = i // spec
+            value = value - flux + jnp.where(north, below, above)
+            diff = pltpu.roll(value, lon - 1, 1) - value
+            slope = minmod(pltpu.roll(diff, 1, 1), diff)
+            g = coef[2, t, p, sub, :] * value + coef[3, t, p, sub, :] * slope
+            upwind = jnp.where(east, pltpu.roll(g, 1, 1), pltpu.roll(g, lon - 1, 1))
+            return (value - g + upwind) * mask_b[i]
+
+        below, flux, held = zero, None, None
+        current = next(values)
+        prior = current
+        for i in range(rows):
+            t = i // spec
+            ahead = next(values) if i + 1 < rows else zero
+            diff = ahead - current
+            g = coef[0, t, p, sub, :] * current + coef[1, t, p, sub, :] * minmod(prior, diff)
+            if i > 0:
+                yield along_row(i - 1, held, flux, below, g)
+                below = flux
+            flux, held, prior, current = g, current, diff, ahead
+        yield along_row(rows - 1, held, flux, below, zero)
+
+    def stream(p, sub, count):
+        values = (cells[p, i, sub, :] for i in range(rows))
+        for _ in range(count):
+            values = substep(p, sub, values)
+        for i, value in enumerate(values):
+            cells[p, i, sub, :] = value
+
     def transport(p):
-        def substep(step, carry):
-            for b in range(pband // 8):
-                sub = slice(b * 8, (b + 1) * 8)
-                north = speed[0, p, sub, :] > 0
-                east = speed[1, p, sub, :] > 0
-                zero = jnp.zeros((8, lon), F32)
-                current = cells[p, 0, sub, :]
-                ahead = cells[p, 1, sub, :]
-                prior_diff = current
-
-                def finish(i, value, below, flux, above):
-                    t = i // spec
-                    value = value - flux + jnp.where(north, below, above)
-                    diff = pltpu.roll(value, lon - 1, 1) - value
-                    slope = minmod(pltpu.roll(diff, 1, 1), diff)
-                    g = coef[2, t, p, sub, :] * value + coef[3, t, p, sub, :] * slope
-                    upwind = jnp.where(east, pltpu.roll(g, 1, 1), pltpu.roll(g, lon - 1, 1))
-                    cells[p, i, sub, :] = (value - g + upwind) * mask_b[i]
-
-                before, flux, held = zero, None, None
-                for i in range(rows):
-                    t = i // spec
-                    diff = ahead - current
-                    slope = minmod(prior_diff, diff)
-                    g = coef[0, t, p, sub, :] * current + coef[1, t, p, sub, :] * slope
-                    if i > 0:
-                        finish(i - 1, held, before, flux, g)
-                        before = flux
-                    flux, held, prior_diff = g, current, diff
-                    current = ahead
-                    ahead = cells[p, i + 2, sub, :] if i + 2 < rows else zero
-                finish(rows - 1, held, before, flux, zero)
-            return carry
-
-        lax.fori_loop(0, SUBSTEPS, substep, 0)
+        count = SUBSTEPS if rows <= 64 else 1
+        for b in range(pband // 8):
+            sub = slice(b * 8, (b + 1) * 8)
+
+            def chain(step, carry):
+                stream(p, sub, count)
+                return carry
+
+            if count == SUBSTEPS:
+                chain(0, 0)
+            else:
+                lax.fori_loop(0, SUBSTEPS, chain, 0)
 
     def nest(p):
         def gather(c):
@@ -372,6 +384,10 @@
         pltpu.make_async_copy(sent, sent, go_send.at[p]).wait()
         sent = cells.at[p, pl.ds(0, n - 1)]
         pltpu.make_async_copy(sent, sent, back_send.at[p]).wait()
+
+
+def masked(value, mask, out):
+    out[...] = value[...] * mask[...]
 
 
 def shards(
@@ -457,7 +473,16 @@
         nest_src.reshape(erows, width),
         nest_into.reshape(erows, width),
     )
-    return (result * own_row).reshape(spectra.shape)
+    blocks = 3 if bins % 24 == 0 else 1
+    block = pl.BlockSpec((bins // blocks, lon), lambda i: (i, 0))
+    return pl.pallas_call(
+        masked,
+        grid=(blocks,),
+        out_shape=jax.ShapeDtypeStruct((bins, lon), F32),
+        in_specs=[block, pl.BlockSpec((1, lon), lambda i: (0, 0))],
+        out_specs=block,
+        compiler_params=pltpu.CompilerParams(vmem_limit_bytes=56 * 1024 * 1024),
+    )(result, own_row).reshape(spectra.shape)
 
 
 def solution(mesh):

time: 32.4 us -> 33.1 us (1.022)
  Pallas kernels: 30.5 us -> 32.9 us
  other arithmetic: 1.77 us -> 0 us
    pallas_call x0 -> x1, Pallas kernels: none -> 2.62 us  [shards(): pl.pallas_call(masked, grid=(blocks,), out_shape=jax.ShapeDtypeStruct((bi...]
    mul x1 -> x0, other arithmetic: 1.77 us -> none  [shards(): return (result * own_row).reshape(spectra.shape)]
where the time goes in v4:
time: 33.1 us; the launch traced here: 32.9 us
  Pallas kernels  32.9 us (99%)
    pallas_call x1, Pallas kernels, shards(): pl.pallas_call(functools.partial(kernel, dims), out_shape=[jax.ShapeDtype...  30.3 us
    pallas_call x1, Pallas kernels, shards(): pl.pallas_call(masked, grid=(blocks,), out_shape=jax.ShapeDtypeStruct((bi...  2.62 us

profile of v4, /device:TPU:0, one launch (start us, length us, event | category | flops | bytes accessed | tf_op | source)
XLA Modules:
  0.0 32.9 jit_solution(1655799467377859095)
XLA Ops:
  0.0 30.3 %shard_map.91 = (f32[768,128]{1,0:T(8,128)}, f32[1,128]{1,0:T(1,128)}) custom-call(f32[768,128]{1,0:T(8,128)} %bitcast.7, bf16[768,768]{1,0:T(8,128)(2,1)} %quad_first.1, bf16[768,768]{1,0:T(8,128)(2,1)} %quad_second.1, bf16[768,768]{1,0:T(8,128)(2,1)} %quad_output.1, s32[8]{0:T(128)} %owner_in.1, s32[4,128]{1,0:T(4,128)} %land_in.1, s32[1,64]{1,0:T(1,128)} %bitcast.8, ...), custom_call_target="tpu_custom_call" | custom-call | flops 905969664 | bytes 4325376 | tf_op jit(solution)/shard_map/pallas_call | solution.py:423
  30.3 2.6 %shard_map.92 = f32[768,128]{1,0:T(8,128)} custom-call(f32[768,128]{1,0:T(8,128)} %get-tuple-element.7.value, f32[1,128]{1,0:T(1,128)} %get-tuple-element.8.mask), custom_call_target="tpu_custom_call" | custom-call | tf_op jit(solution)/shard_map/pallas_call | solution.py:478

commit v5 on v4

--- a/solution.py
+++ b/solution.py
@@ -41,7 +41,7 @@
 def kernel(
     dims,
     spectra, quad_first, quad_second, quad_output, owner_in, land_in, dest_in, src_in, into_in,
-    out, out_mask,
+    out,
     owner, land, dest, src, into, field, w1, w2, w3, outbox, cells, inbox, sums, meta, ent, mask_b, inv_b, coef, speed, oh_src, oh_dst, gathered,
     load_sem, meta_send, meta_recv, go_send, go_recv, back_send, back_recv,
 ):
@@ -373,8 +373,7 @@
     product = (one * two).astype(BF16)
     for p in range(parts):
         rows_p = slice(p * width_p, (p + 1) * width_p)
-        out[rows_p, :] = field[rows_p, :] + third(product, p)
-    out_mask[...] = own_mask
+        out[rows_p, :] = (field[rows_p, :] + third(product, p)) * own_mask
 
     pltpu.make_async_copy(
         meta.at[pl.ds(0, tiles - 1)], meta.at[pl.ds(0, tiles - 1)], meta_send
@@ -384,10 +383,6 @@
         pltpu.make_async_copy(sent, sent, go_send.at[p]).wait()
         sent = cells.at[p, pl.ds(0, n - 1)]
         pltpu.make_async_copy(sent, sent, back_send.at[p]).wait()
-
-
-def masked(value, mask, out):
-    out[...] = value[...] * mask[...]
 
 
 def shards(
@@ -420,11 +415,11 @@
     hbm = pl.BlockSpec(memory_space=pltpu.HBM)
     V = pltpu.VMEM
     dma = pltpu.SemaphoreType.DMA
-    result, own_row = pl.pallas_call(
+    result = pl.pallas_call(
         functools.partial(kernel, dims),
-        out_shape=[jax.ShapeDtypeStruct((bins, lon), F32), jax.ShapeDtypeStruct((1, lon), F32)],
+        out_shape=jax.ShapeDtypeStruct((bins, lon), F32),
         in_specs=[hbm] * 9,
-        out_specs=[vmem, vmem],
+        out_specs=vmem,
         scratch_shapes=[
             pltpu.SMEM(owner_map.shape, jnp.int32),
             V(land_mask.shape, jnp.int32),
@@ -473,16 +468,7 @@
         nest_src.reshape(erows, width),
         nest_into.reshape(erows, width),
     )
-    blocks = 3 if bins % 24 == 0 else 1
-    block = pl.BlockSpec((bins // blocks, lon), lambda i: (i, 0))
-    return pl.pallas_call(
-        masked,
-        grid=(blocks,),
-        out_shape=jax.ShapeDtypeStruct((bins, lon), F32),
-        in_specs=[block, pl.BlockSpec((1, lon), lambda i: (0, 0))],
-        out_specs=block,
-        compiler_params=pltpu.CompilerParams(vmem_limit_bytes=56 * 1024 * 1024),
-    )(result, own_row).reshape(spectra.shape)
+    return result.reshape(spectra.shape)
 
 
 def solution(mesh):

time: 33.1 us -> 32.2 us (0.973)
  Pallas kernels: 32.9 us -> 30.3 us
  local copies, waits for them, and re-layouts: 0 us -> 1.77 us
    pallas_call x2 -> x1, Pallas kernels: 32.9 us -> 30.3 us  [shards(): pl.pallas_call(functools.partial(kernel, dims), out_shape=jax.ShapeDtypeS...]
    unnamed x0 -> x1, local copies, waits for them, and re-layouts: none -> 1.77 us
where the time goes in v5:
time: 32.2 us; the launch traced here: 32 us
  Pallas kernels  30.3 us (94%)
  local copies, waits for them, and re-layouts  1.77 us (5%)
    pallas_call x1, Pallas kernels, shards(): pl.pallas_call(functools.partial(kernel, dims), out_shape=jax.ShapeDtypeS...  30.3 us
    unnamed x1, local copies, waits for them, and re-layouts  1.77 us

profile of v5, /device:TPU:0, one launch (start us, length us, event | category | flops | bytes accessed | tf_op | source)
XLA Modules:
  0.0 32.0 jit_solution(18032932986227570705)
XLA Ops:
  0.0 30.3 %shard_map.91 = f32[768,128]{1,0:T(8,128)} custom-call(f32[768,128]{1,0:T(8,128)} %bitcast.8, bf16[768,768]{1,0:T(8,128)(2,1)} %quad_first.1, bf16[768,768]{1,0:T(8,128)(2,1)} %quad_second.1, bf16[768,768]{1,0:T(8,128)(2,1)} %quad_output.1, s32[8]{0:T(128)} %owner_in.1, s32[4,128]{1,0:T(4,128)} %land_in.1, s32[1,64]{1,0:T(1,128)} %bitcast.9, ...), custom_call_target="tpu_custom_call" | custom-call | flops 905969664 | bytes 4325376 | tf_op jit(solution)/shard_map/pallas_call | solution.py:418
  30.3 1.8 %copy.12 = f32[768,1,128]{2,1,0:T(1,128)} copy(f32[768,1,128]{2,1,0:T(1,128)} %bitcast.7) | data formatting | bytes 786432
